TPU v7x, 32 devices: a whole 2x2x4 slice. The times are simulated.
32 devices in a mesh: groups: 2 (over y), stores: 4 (over z), weeks: 4 (over x, core).
Axes of the slice: x: 2, y: 2, z: 4, core: 2. Of those that a mesh axis runs over, the one named last changes fastest.
Arguments:
- outcomes: float32 [1024, 8192], P(('groups', 'weeks'), 'stores'), parts along dimension 0, may hold values from -40 to 40
- observed_mask: int32 [1024, 8192], P(('groups', 'weeks'), 'stores'), parts along dimension 0, may hold values 0 or 1
- store_region: int32 [8192], P('stores'), may hold values from 0 to 15
- store_factor: float32 [16384, 128], P(('groups', 'stores')), parts along dimension 0, may hold values from -0.5 to 0.5
- week_factor: float32 [1024, 128], P(('groups', 'weeks')), parts along dimension 0, may hold values from -6 to 6
Outputs:
- imputed: float32 [1024, 8192], P(('groups', 'weeks'), 'stores'), parts along dimension 0
- store_loadings: float32 [16384, 128], P(('groups', 'stores')), parts along dimension 0
- week_loadings: float32 [1024, 128], P(('groups', 'weeks')), parts along dimension 0
There are 2 independent parts, one for each index of `groups`. A program takes and returns all parts, laid end to end along the dimension named above; an argument that names none is the same for every part. Nothing has to cross between parts.
All inputs are finite; a program needn't handle non-finite values. No bound on the sum of `observed_mask` on one device may be relied on, other than what follows from the above.
Results may differ from a plain program's by a relative error of at most 0.00013.
Values sent between devices are 32-bit elements; how exact they have to be, the bound alone decides.
A program may use at most 64 MiB of HBM per device.

v0:
```python
import jax
import jax.numpy as jnp
from jax import lax
from jax.sharding import PartitionSpec as P

REGIONS = 16
ITERS = 2


PRECISE = lax.Precision.HIGHEST
RIDGE_WEIGHT = 8.0


def gram_inverse(gram):
    identity = jnp.eye(gram.shape[0], dtype=gram.dtype)
    lower_factor = jnp.linalg.cholesky(gram + RIDGE_WEIGHT * identity)
    lower_inverse = lax.linalg.triangular_solve(lower_factor, identity, left_side=True, lower=True)
    return jnp.dot(lower_inverse.T, lower_inverse, precision=PRECISE)


def masked_residual(observed, centered, factor_week, factor_store):
    return observed * (centered - jnp.dot(factor_week, factor_store.T, precision=PRECISE))


def on_device(outcomes, observed_mask, store_region, store_factor, week_factor):
    observed = observed_mask.astype(jnp.float32)
    onehot = (store_region[:, None] == jnp.arange(REGIONS, dtype=jnp.int32)[None, :]).astype(
        jnp.float32
    )
    region_total = jnp.dot(observed * outcomes, onehot, precision=PRECISE)
    region_count = jnp.dot(observed, onehot, precision=PRECISE)
    region_total, region_count = lax.psum((region_total, region_count), "stores")
    region_effect = region_total / (region_count + 1.0)
    region_cells = jnp.dot(region_effect, onehot.T, precision=PRECISE)
    store_total = jnp.sum(observed * (outcomes - region_cells), axis=0)
    store_count = jnp.sum(observed, axis=0)
    store_total, store_count = lax.psum((store_total, store_count), "weeks")
    store_effect = store_total / (store_count + 1.0)
    centered = outcomes - region_cells - store_effect[None, :]
    factor_store = store_factor
    factor_week = week_factor
    for iteration in range(ITERS):
        store_gram = lax.psum(jnp.dot(factor_store.T, factor_store, precision=PRECISE), "stores")
        residual = masked_residual(observed, centered, factor_week, factor_store)
        product = lax.psum(jnp.dot(residual, factor_store, precision=PRECISE), "stores")
        factor_week = jnp.dot(
            product + jnp.dot(factor_week, store_gram, precision=PRECISE),
            gram_inverse(store_gram),
            precision=PRECISE,
        )
        residual = masked_residual(observed, centered, factor_week, factor_store)
        local_product = jnp.einsum("ws,wr->sr", residual, factor_week, precision=PRECISE)
        product, week_gram = lax.psum(
            (local_product, jnp.dot(factor_week.T, factor_week, precision=PRECISE)), "weeks"
        )
        factor_store = jnp.dot(
            product + jnp.dot(factor_store, week_gram, precision=PRECISE),
            gram_inverse(week_gram),
            precision=PRECISE,
        )
    imputed = (
        region_cells
        + store_effect[None, :]
        + jnp.dot(factor_week, factor_store.T, precision=PRECISE)
    )
    return (imputed, factor_store, factor_week)


def solution(mesh):
    placed = (
        P(("groups", "weeks"), "stores"),
        P(("groups", "weeks"), "stores"),
        P("stores"),
        P(("groups", "stores"), None),
        P(("groups", "weeks"), None),
    )
    return jax.shard_map(
        on_device,
        mesh=mesh,
        in_specs=placed,
        out_specs=(
            P(("groups", "weeks"), "stores"),
            P(("groups", "stores"), None),
            P(("groups", "weeks"), None),
        ),
        check_vma=False,
    )
```

profile of v0, /device:TPU:0, one launch (start us, length us, event | category | flops | bytes accessed | tf_op | source)
XLA Modules:
  0.0 329.0 jit_solution(18331463596920854841)
XLA Ops:
  7.2 2.2 convolution_bitcast_fusion.2
  11.6 2.4 fusion.39
  14.1 23.1 %all-reduce.3 = (f32[128,16]{1,0:T(8,128)S(1)}, f32[128,16]{1,0:T(8,128)S(1)}) all-reduce(f32[128,16]{1,0:T(8,128)S(1)} %fusion.7, f32[128,16]{1,0:T(8,128)S(1)} %convolution_bitcast_fusion.2), channel_id=1, replica_groups=mesh['groups'=2,'stores'=4,'weeks'=4] {'stores'}, use_global_device_ids=true, to_apply=%region_0.0 | all-reduce | flops 4096 | bytes 32768 | tf_op jit(solution)/shard_map/psum | solution.py:32
  37.2 3.1 convert_reduce_fusion
  40.3 10.1 %all-reduce = (f32[2048]{0:T(1024)S(1)}, f32[2048]{0:T(1024)S(1)}) all-reduce(f32[2048]{0:T(1024)S(1)} %get-tuple-element.6, f32[2048]{0:T(1024)S(1)} %get-tuple-element.5), channel_id=1, replica_groups=mesh['groups'=2,'stores'=4,'weeks'=4] {'weeks'}, use_global_device_ids=true, to_apply=%region_3.0 | all-reduce | flops 4096 | bytes 32768 | tf_op jit(solution)/shard_map/psum | solution.py:37
  54.0 32.6 %all-reduce.17.cloned.1.call-done = (f32[128,128]{1,0:T(8,128)}, f32[128,128]{0,1:T(8,128)}) async-done(((f32[128,128]{1,0:T(8,128)}, f32[128,128]{0,1:T(8,128)}), (f32[128,128]{1,0:T(8,128)}, f32[128,128]{0,1:T(8,128)})) %all-reduce.17.cloned.1.call-update) | async-done | bytes 131088 | tf_op jit(solution)/shard_map/psum | solution.py:45
  88.0 11.7 %cholesky.74 = f32[128,128]{1,0:T(8,128)S(1)} custom-call(f32[128,128]{1,0:T(8,128)S(1)} %fusion.33), custom_call_target="Cholesky" | custom-call | tf_op jit(solution)/shard_map/jit(cholesky)/cholesky | solution.py:16
  101.0 9.8 %custom-call.8 = f32[1,128,128]{1,2,0:T(8,128)S(1)} custom-call(f32[1,128,128]{2,1,0:T(8,128)S(1)} %fusion.22), custom_call_target="InvertDiagBlocksLowerTriangular" | custom-call | tf_op jit(solution)/shard_map/triangular_solve/custom-call.0 | solution.py:17
  113.8 2.8 fusion.42
  116.8 36.5 %all-reduce.13.cloned.1.call-done = (f32[2048,128]{1,0:T(8,128)}, f32[128,128]{0,1:T(8,128)}) async-done(((f32[2048,128]{1,0:T(8,128)}, f32[128,128]{0,1:T(8,128)}), (f32[2048,128]{1,0:T(8,128)}, f32[128,128]{0,1:T(8,128)})) %all-reduce.13.cloned.1.call-update) | async-done | bytes 1114128 | tf_op jit(solution)/shard_map/psum | solution.py:53
  154.2 3.2 fusion
  157.5 11.7 %cholesky.85 = f32[128,128]{1,0:T(8,128)S(1)} custom-call(f32[128,128]{1,0:T(8,128)S(1)} %fusion.31), custom_call_target="Cholesky" | custom-call | tf_op jit(solution)/shard_map/jit(cholesky)/cholesky | solution.py:16
  170.6 9.8 %custom-call.9 = f32[1,128,128]{1,2,0:T(8,128)S(1)} custom-call(f32[1,128,128]{2,1,0:T(8,128)S(1)} %fusion.23), custom_call_target="InvertDiagBlocksLowerTriangular" | custom-call | tf_op jit(solution)/shard_map/triangular_solve/custom-call.0 | solution.py:17
  181.0 2.2 fusion.45
  183.2 2.4 fusion.47
  189.0 34.9 %all-reduce.15.cloned.1.call-done = (f32[128,128]{1,0:T(8,128)}, f32[128,128]{0,1:T(8,128)}) async-done(((f32[128,128]{1,0:T(8,128)}, f32[128,128]{0,1:T(8,128)}), (f32[128,128]{1,0:T(8,128)}, f32[128,128]{0,1:T(8,128)})) %all-reduce.15.cloned.1.call-update) | async-done | bytes 131088 | tf_op jit(solution)/shard_map/psum | solution.py:45
  225.2 11.7 %cholesky.96 = f32[128,128]{1,0:T(8,128)S(1)} custom-call(f32[128,128]{1,0:T(8,128)S(1)} %fusion.29), custom_call_target="Cholesky" | custom-call | tf_op jit(solution)/shard_map/jit(cholesky)/cholesky | solution.py:16
  238.3 9.8 %custom-call.10 = f32[1,128,128]{1,2,0:T(8,128)S(1)} custom-call(f32[1,128,128]{2,1,0:T(8,128)S(1)} %fusion.24), custom_call_target="InvertDiagBlocksLowerTriangular" | custom-call | tf_op jit(solution)/shard_map/triangular_solve/custom-call.0 | solution.py:17
  248.9 2.5 fusion.1
  252.3 2.8 fusion.50
  255.1 36.7 %all-reduce.11.cloned.1.call-done = (f32[2048,128]{1,0:T(8,128)}, f32[128,128]{0,1:T(8,128)}) async-done(((f32[2048,128]{1,0:T(8,128)}, f32[128,128]{0,1:T(8,128)}), (f32[2048,128]{1,0:T(8,128)}, f32[128,128]{0,1:T(8,128)})) %all-reduce.11.cloned.1.call-update) | async-done | bytes 1114128 | tf_op jit(solution)/shard_map/psum | solution.py:53
  292.7 2.2 convolution_add_fusion.1
  295.1 11.9 %cholesky.107 = f32[128,128]{1,0:T(8,128)S(1)} custom-call(f32[128,128]{1,0:T(8,128)S(1)} %fusion.27), custom_call_target="Cholesky" | custom-call | tf_op jit(solution)/shard_map/jit(cholesky)/cholesky | solution.py:16
  308.4 9.8 %custom-call.11 = f32[1,128,128]{1,2,0:T(8,128)S(1)} custom-call(f32[1,128,128]{2,1,0:T(8,128)S(1)} %fusion.25), custom_call_target="InvertDiagBlocksLowerTriangular" | custom-call | tf_op jit(solution)/shard_map/triangular_solve/custom-call.0 | solution.py:17
  (85 shorter events, 28.3 us)
Async XLA Ops:
  7.2 4.5 %copy-start = (f32[2048,128]{1,0:T(8,128)S(1)}, f32[2048,128]{1,0:T(8,128)}, u32[]{:S(2)}) copy-start(f32[2048,128]{1,0:T(8,128)} %param.11) | copy-start | bytes 3145732
  7.2 2.3 copy-start.1
  7.2 2.3 copy-start.12
  7.2 79.4 %all-reduce.17.cloned.1.call-start = ((), (), s32[]{:S(2)}) async-start(), calls=%async_computation.3 | async-start | bytes 262144 | tf_op jit(solution)/shard_map/psum | solution.py:45
  37.2 13.2 %copy-start.11 = (f32[128,128]{1,0:T(8,128)S(1)}, f32[128,128]{1,0:T(8,128)}, u32[]{:S(2)}) copy-start(f32[128,128]{1,0:T(8,128)} %param.12) | copy-start | bytes 196612
  40.3 72.3 %copy-start.2 = (f32[128,2048]{1,0:T(8,128)}, f32[128,2048]{1,0:T(8,128)S(1)}, u32[]{:S(2)}) copy-start(f32[128,2048]{1,0:T(8,128)S(1)} %get-tuple-element.19) | copy-start | bytes 3145732
  53.5 99.8 %all-reduce.13.cloned.1.call-start = ((), (), s32[]{:S(2)}) async-start(), calls=%async_computation.1 | async-start | bytes 2228224 | tf_op jit(solution)/shard_map/psum | solution.py:53
  86.6 0.9 copy-start.10
  86.6 0.9 copy-start.14
  116.6 107.3 %all-reduce.15.cloned.1.call-start = ((), (), s32[]{:S(2)}) async-start(), calls=%async_computation.2 | async-start | bytes 262144 | tf_op jit(solution)/shard_map/psum | solution.py:45
  153.3 0.9 copy-start.7
  183.2 2.5 copy-start.3
  188.9 102.8 %all-reduce.11.cloned.1.call-start = ((), (), s32[]{:S(2)}) async-start(), calls=%async_computation | async-start | bytes 2228224 | tf_op jit(solution)/shard_map/psum | solution.py:53
  223.9 0.9 copy-start.9
  223.9 0.9 copy-start.13
  248.9 70.9 %copy-start.6 = (f32[128,128]{1,0:T(8,128)}, f32[128,128]{1,0:T(8,128)S(1)}, u32[]{:S(2)}) copy-start(f32[128,128]{1,0:T(8,128)S(1)} %fusion.49) | copy-start | bytes 196612
  291.8 0.9 copy-start.8
  318.8 1.2 copy-start.5
  319.8 2.3 copy-start.4
Sparse Core Ops, SparseCore 0:
  53.6 32.9 all-reduce.16
  116.7 36.5 all-reduce.12
  189.1 34.7 all-reduce.14
  255.2 36.5 all-reduce.10
where the time goes:
time: 335 us; the launch traced here: 329 us
  waiting for transfers between devices  141 us (42%)
  other arithmetic  95.4 us (28%)
  matrix products  43.5 us (13%)
  blocking collectives  33.2 us (10%)
  between operations  14.7 us (4%)
    psum x2, waiting for transfers between devices, on_device(): lax.psum((local_product, jnp.dot(factor_week.T, factor_week, precision=PR...  73.2 us
    psum x2, waiting for transfers between devices, on_device(): lax.psum(jnp.dot(residual, factor_store, precision=PRECISE), 'stores')  67.5 us
    another operation x12, other arithmetic, gram_inverse(): lower_factor = jnp.linalg.cholesky(gram + RIDGE_WEIGHT * identity)  49.8 us
    another operation x8, other arithmetic, gram_inverse(): lax.linalg.triangular_solve(lower_factor, identity, left_side=True, lower...  41.9 us
    psum x1, blocking collectives, on_device(): lax.psum((region_total, region_count), 'stores')  23.1 us
    psum x1, blocking collectives, on_device(): store_total, store_count = lax.psum((store_total, store_count), 'weeks')  10.1 us
  transfers between devices with their start and end apart: 4, of which 4 were waited for; matrix products, arithmetic and copies ran while one was open for 0% of the time, Pallas kernels for 0%

commit v1 on v0

v1 whole, which is shorter than its diff:
```python
import functools

import jax
import jax.numpy as jnp
from jax import lax
from jax.experimental import pallas as pl
from jax.experimental.pallas import tpu as pltpu
from jax.sharding import PartitionSpec as P

REGIONS = 16
ITERS = 2
RIDGE_WEIGHT = 8.0
PANEL = 16
MESH = pl.DeviceIdType.MESH
PRECISE = lax.Precision.HIGHEST


def dot(a, b, ca=1, cb=0):
    return lax.dot_general(
        a, b, (((ca,), (cb,)), ((), ())), precision=PRECISE, preferred_element_type=jnp.float32
    )


def inverse(gram, work):
    rank = gram.shape[0]
    row_at = lax.broadcasted_iota(jnp.int32, (rank, rank), 0)
    lane_at = lax.broadcasted_iota(jnp.int32, (rank, rank), 1)
    work[...] = gram + jnp.where(row_at == lane_at, RIDGE_WEIGHT, 0.0)
    panel_row = lax.broadcasted_iota(jnp.int32, (PANEL, rank), 0)
    panel_lane = lax.broadcasted_iota(jnp.int32, (PANEL, rank), 1)

    def step(_, carry):
        matrix = work[...]
        panel = matrix[:PANEL, :]
        for j in range(PANEL):
            pivot = 1.0 / panel[j : j + 1, j : j + 1]
            row = jnp.where(panel_lane[:1] == j, pivot, panel[j : j + 1, :] * pivot)
            column = panel[:, j : j + 1]
            cleared = jnp.where(panel_lane == j, 0.0, panel)
            panel = jnp.where(panel_row == j, row, cleared - column * row)
        rest = matrix[PANEL:, :]
        kept = jnp.where(lane_at[PANEL:] < PANEL, 0.0, rest)
        rest = kept - dot(rest[:, :PANEL], panel)
        work[...] = pltpu.roll(jnp.concatenate([rest, panel], axis=0), rank - PANEL, 1)
        return carry

    lax.fori_loop(0, rank // PANEL, step, 0)
    return work[...]


class Sum:
    def __init__(self, axis, n, me, refs):
        self.axis, self.n, self.me = axis, n, me
        self.send, self.part, self.full, self.sems = refs
        self.rows = self.send.shape[0] // n
        self.direct = self.rows < 8

    @staticmethod
    def scratch(n, rank):
        rows = rank // n
        part = (n, rank, rank) if rows < 8 else (n, rows, rank)
        return [
            pltpu.VMEM((rank, rank), jnp.float32),
            pltpu.VMEM(part, jnp.float32),
            pltpu.VMEM((rank, rank), jnp.float32),
            pltpu.SemaphoreType.DMA((4, n)),
        ]

    def block(self, ref, owner):
        return ref.at[pl.ds(pl.multiple_of(owner * self.rows, 8), self.rows)]

    def first(self, j):
        peer = lax.rem(self.me + j, self.n)
        source = self.send if self.direct else self.block(self.send, peer)
        return pltpu.make_async_remote_copy(
            source, self.part.at[j], self.sems.at[0, j], self.sems.at[1, j],
            device_id={self.axis: peer}, device_id_type=MESH,
        )

    def second(self, j, arriving):
        owner = lax.rem(self.me + self.n - j, self.n) if arriving else self.me
        peer = lax.rem(self.me + j, self.n)
        block = self.block(self.full, owner)
        return pltpu.make_async_remote_copy(
            block, block, self.sems.at[2, j], self.sems.at[3, j],
            device_id={self.axis: peer}, device_id_type=MESH,
        )

    def start(self, value):
        self.send[...] = value
        for j in range(1, self.n):
            self.first(j).start()

    def spread(self):
        if self.direct:
            return
        total = self.block(self.send, self.me)[...]
        for j in range(1, self.n):
            self.first(j).wait_recv()
            total = total + self.part[j]
        self.block(self.full, self.me)[...] = total
        for j in range(1, self.n):
            self.second(j, False).start()

    def result(self):
        if not self.direct:
            for j in range(1, self.n):
                self.second(j, True).wait_recv()
            return self.full[...]
        for j in range(1, self.n):
            self.first(j).wait_recv()
        self.part[0] = self.send[...]

        def body(t, total):
            return total + self.part[lax.rem(self.n - t + self.me, self.n)]

        return lax.fori_loop(0, self.n, body, jnp.zeros(self.send.shape, jnp.float32))

    def drain(self):
        for j in range(1, self.n):
            self.first(j).wait_send()
            if not self.direct:
                self.second(j, False).wait_send()


def fused(nz, nw, n_sum, *refs):
    (outcomes, mask, region, a_first, b_first, imputed, a_out, b_out) = refs[:8]
    refs = refs[8:]
    (onehot, obs, cent, base, pred, obs_t, cent_t, work, region_buf, store_buf, effect_row,
     region_sems, store_sems) = refs[:13]
    refs = refs[13:]
    (sib_send, sib_recv, x_send, x_recv, own, a_all, sib_sems, x_sems, ax_sems, as_sems) = refs[:10]
    refs = refs[10:]
    z = lax.axis_index("stores")
    w = lax.axis_index("weeks")
    sums = []
    for k in range(4 * ITERS - ITERS):
        over_z = k % 3 < 2
        group = refs[4 * k : 4 * k + 4]
        sums.append(Sum("stores", nz, z, group) if over_z else Sum("weeks", nw, w, group))
    weeks, stores = outcomes.shape
    rank = b_first.shape[1]
    core, chip, chips = lax.rem(w, 2), w // 2, nw // 2
    half = stores // 2
    sub = half // chips
    tile = 128
    per_sub = sub // tile
    n_tiles = half // tile
    n_away = n_tiles - per_sub
    wide = stores // 4

    barrier = pltpu.get_barrier_semaphore()
    for j in range(1, nz):
        pl.semaphore_signal(barrier, device_id={"stores": lax.rem(z + j, nz)}, device_id_type=MESH)
    for j in range(1, nw):
        pl.semaphore_signal(barrier, device_id={"weeks": lax.rem(w + j, nw)}, device_id_type=MESH)

    onehot[...] = (
        lax.broadcasted_iota(jnp.int32, (REGIONS, stores), 0) == region[...]
    ).astype(jnp.float32)
    obs[...] = mask[...].astype(jnp.float32)
    total = dot(onehot[...], obs[...] * outcomes[...], 1, 1)
    count = dot(onehot[...], obs[...], 1, 1)
    region_buf[0] = jnp.concatenate([total, count], axis=0)
    pl.semaphore_wait(barrier, nz + nw - 2)

    def region_copy(j):
        return pltpu.make_async_remote_copy(
            region_buf.at[0], region_buf.at[j], region_sems.at[0, j], region_sems.at[1, j],
            device_id={"stores": lax.rem(z + j, nz)}, device_id_type=MESH,
        )

    for j in range(1, nz):
        region_copy(j).start()

    def gram_of(ref):
        def body(t, total):
            block = ref[pl.ds(pl.multiple_of(t * 256, 256), 256), :]
            return total + dot(block.T, block)

        return lax.fori_loop(0, stores // 256, body, jnp.zeros((rank, rank), jnp.float32))

    sums[0].start(gram_of(a_first))

    for j in range(1, nz):
        region_copy(j).wait_recv()

    def add_region(t, total):
        return total + region_buf[lax.rem(z - t + nz, nz)]

    sums_region = lax.fori_loop(
        0, nz, add_region, jnp.zeros(region_buf.shape[1:], jnp.float32)
    )
    effect = (sums_region[:REGIONS] / (sums_region[REGIONS:] + 1.0)).T
    base[...] = dot(effect, onehot[...])
    store_total = jnp.sum(obs[...] * (outcomes[...] - base[...]), axis=0, keepdims=True)
    store_count = jnp.sum(obs[...], axis=0, keepdims=True)
    for q in range(4):
        store_buf[0, q : q + 1, :] = store_total[:, q * wide : (q + 1) * wide]
        store_buf[0, q + 4 : q + 5, :] = store_count[:, q * wide : (q + 1) * wide]

    def store_copy(j):
        return pltpu.make_async_remote_copy(
            store_buf.at[0], store_buf.at[j], store_sems.at[0, j], store_sems.at[1, j],
            device_id={"weeks": lax.rem(w + j, nw)}, device_id_type=MESH,
        )

    for j in range(1, nw):
        store_copy(j).start()
    sums[0].spread()

    def predict(b_value, ref):
        def body(t, carry):
            at = pl.ds(pl.multiple_of(t * 256, 256), 256)
            pred[:, at] = dot(b_value, ref[at, :], 1, 1)
            return carry

        lax.fori_loop(0, stores // 256, body, 0)

    predict(b_first[...], a_first)

    def turn(source, target):
        def body(t, carry):
            at = pl.ds(pl.multiple_of(t * 128, 128), 128)
            target[at, :] = source[:, at].T
            return carry

        lax.fori_loop(0, stores // 128, body, 0)

    turn(obs, obs_t)
    for j in range(1, nw):
        store_copy(j).wait_recv()

    def add_store(t, total):
        return total + store_buf[lax.rem(w - t + nw, nw)]

    sums_store = lax.fori_loop(0, nw, add_store, jnp.zeros(store_buf.shape[1:], jnp.float32))
    effect_s = sums_store[:4] / (sums_store[4:] + 1.0)
    for q in range(4):
        effect_row[:, q * wide : (q + 1) * wide] = effect_s[q : q + 1]
    base[...] = base[...] + effect_row[...]
    cent[...] = obs[...] * (outcomes[...] - base[...])

    b_value = b_first[...]
    a_ref = a_first
    for it in range(ITERS):
        sum_gram, sum_product, sum_week = sums[3 * it : 3 * it + 3]
        if it > 0:
            sum_gram.start(gram_of(a_ref))
            predict(b_value, a_ref)

        def product_step(t, total):
            at = pl.ds(pl.multiple_of(t * 256, 256), 256)
            residual = cent[:, at] - obs[:, at] * pred[:, at]
            return total + dot(residual, a_ref[at, :])

        product = lax.fori_loop(
            0, stores // 256, product_step, jnp.zeros((weeks, rank), jnp.float32)
        )
        if weeks < rank:
            product = jnp.concatenate(
                [product, jnp.zeros((rank - weeks, rank), jnp.float32)], axis=0
            )
        sum_product.start(product)
        if it > 0:
            sum_gram.spread()
        gram = sum_gram.result()
        if it == 0:
            turn(cent, cent_t)
        sum_product.spread()
        inv = inverse(gram, work)
        product = sum_product.result()[:weeks]
        b_value = dot(product + dot(b_value, gram), inv)

        sum_week.start(dot(b_value.T, b_value))

        def rows_of(i):
            to = lax.rem(chip + 1 + i // per_sub, chips)
            return pl.multiple_of(to * sub + lax.rem(i, per_sub) * tile, tile)

        def local_product(row):
            at = pl.ds(pl.multiple_of(row, tile), tile)
            predicted = dot(a_ref[at, :], b_value, 1, 1)
            return dot(cent_t[at, :] - obs_t[at, :] * predicted, b_value)

        def sib_copy(i):
            at = pl.ds(rows_of(i), tile)
            return pltpu.make_async_remote_copy(
                sib_send.at[it, at], sib_recv.at[it, at],
                sib_sems.at[it, 0, i], sib_sems.at[it, 1, i],
                device_id={"weeks": chip * 2 + 1 - core}, device_id_type=MESH,
            )

        def x_copy(i):
            to = lax.rem(chip + 1 + i // per_sub, chips)
            return pltpu.make_async_remote_copy(
                x_send.at[it, pl.ds(pl.multiple_of(i * tile, tile), tile)],
                x_recv.at[it, pl.ds(pl.multiple_of(i * tile, tile), tile)],
                x_sems.at[it, 0, i], x_sems.at[it, 1, i],
                device_id={"weeks": to * 2 + core}, device_id_type=MESH,
            )

        def to_sibling(i, carry):
            sib_send[it, pl.ds(rows_of(i), tile)] = local_product((1 - core) * half + rows_of(i))
            sib_copy(i).start()
            return carry

        def chip_sum(i):
            mine = local_product(core * half + rows_of(i))
            sib_copy(i).wait_recv()
            theirs = sib_recv[it, pl.ds(rows_of(i), tile)]
            return mine + theirs

        def to_chips(i, carry):
            x_send[it, pl.ds(pl.multiple_of(i * tile, tile), tile)] = chip_sum(i)
            x_copy(i).start()
            return carry

        def keep(i, carry):
            own[pl.ds(pl.multiple_of((i - n_away) * tile, tile), tile)] = chip_sum(i)
            return carry

        lax.fori_loop(0, n_away, to_sibling, 0)
        lax.fori_loop(0, n_away, to_chips, 0)
        sum_week.spread()
        lax.fori_loop(n_away, n_tiles, to_sibling, 0)
        lax.fori_loop(n_away, n_tiles, keep, 0)
        week_gram = sum_week.result()
        inv = inverse(week_gram, work)

        def a_copy_x(d, q, arriving):
            owner = lax.rem(chip + chips - d, chips) if arriving else chip
            at = pl.ds(pl.multiple_of(core * half + owner * sub + q * tile, tile), tile)
            return pltpu.make_async_remote_copy(
                a_all.at[it, at], a_all.at[it, at],
                ax_sems.at[it, 0, d, q], ax_sems.at[it, 1, d, q],
                device_id={"weeks": lax.rem(chip + d, chips) * 2 + core}, device_id_type=MESH,
            )

        def a_copy_sib(d, q, arriving):
            owner = lax.rem(chip + chips - d, chips)
            part = 1 - core if arriving else core
            at = pl.ds(pl.multiple_of(part * half + owner * sub + q * tile, tile), tile)
            return pltpu.make_async_remote_copy(
                a_all.at[it, at], a_all.at[it, at],
                as_sems.at[it, 0, d, q], as_sems.at[it, 1, d, q],
                device_id={"weeks": chip * 2 + 1 - core}, device_id_type=MESH,
            )

        def update(q, carry):
            at = pl.ds(pl.multiple_of(q * tile, tile), tile)
            total = own[at]
            for d in range(1, chips):
                i = (d - 1) * per_sub + q
                x_copy(i).wait_recv()
                total = total + x_recv[it, pl.ds(pl.multiple_of(i * tile, tile), tile)]
            rows = pl.ds(pl.multiple_of(core * half + chip * sub + q * tile, tile), tile)
            a_all[it, rows] = dot(total + dot(a_ref[rows, :], week_gram), inv)
            for d in range(1, chips):
                a_copy_x(d, q, False).start()
            a_copy_sib(0, q, False).start()
            return carry

        def forward(q, carry):
            for d in range(1, chips):
                a_copy_x(d, q, True).wait_recv()
                a_copy_sib(d, q, False).start()
            return carry

        def arrive(q, carry):
            for d in range(chips):
                a_copy_sib(d, q, True).wait_recv()
            return carry

        lax.fori_loop(0, per_sub, update, 0)
        lax.fori_loop(0, per_sub, forward, 0)
        lax.fori_loop(0, per_sub, arrive, 0)

        def drain_tiles(i, carry):
            sib_copy(i).wait_send()
            return carry

        def drain_away(i, carry):
            x_copy(i).wait_send()
            return carry

        def drain_rows(q, carry):
            for d in range(chips):
                if d > 0:
                    a_copy_x(d, q, False).wait_send()
                a_copy_sib(d, q, False).wait_send()
            return carry

        lax.fori_loop(0, n_tiles, drain_tiles, 0)
        lax.fori_loop(0, n_away, drain_away, 0)
        lax.fori_loop(0, per_sub, drain_rows, 0)
        a_ref = a_all.at[it]

    b_out[...] = b_value

    def finish(t, carry):
        at = pl.ds(pl.multiple_of(t * 256, 256), 256)
        block = a_ref[at, :]
        a_out[at, :] = block
        imputed[:, at] = base[:, at] + dot(b_value, block, 1, 1)
        return carry

    lax.fori_loop(0, stores // 256, finish, 0)
    for j in range(1, nz):
        region_copy(j).wait_send()
    for j in range(1, nw):
        store_copy(j).wait_send()
    for item in sums:
        item.drain()


def on_device(nz, nw, outcomes, observed_mask, store_region, store_factor, week_factor):
    weeks, stores = outcomes.shape
    rank = week_factor.shape[1]
    chips = nw // 2
    half = stores // 2
    n_tiles = half // 128
    per_sub = n_tiles // chips
    away = max(half - half // chips, 128)
    vmem = lambda *shape: pltpu.VMEM(shape, jnp.float32)
    sems = lambda *shape: pltpu.SemaphoreType.DMA(shape)
    scratch = [
        vmem(REGIONS, stores),
        vmem(weeks, stores), vmem(weeks, stores), vmem(weeks, stores), vmem(weeks, stores),
        vmem(stores, weeks), vmem(stores, weeks),
        vmem(rank, rank),
        vmem(nz, 2 * REGIONS, weeks), vmem(nw, 8, stores // 4), vmem(1, stores),
        sems(2, nz), sems(2, nw),
        vmem(ITERS, half, rank), vmem(ITERS, half, rank),
        vmem(ITERS, away, rank), vmem(ITERS, away, rank),
        vmem(half // chips, rank),
        vmem(ITERS, stores, rank),
        sems(ITERS, 2, n_tiles), sems(ITERS, 2, n_tiles),
        sems(ITERS, 2, chips, per_sub), sems(ITERS, 2, chips, per_sub),
    ]
    for _ in range(ITERS):
        scratch += Sum.scratch(nz, rank) + Sum.scratch(nz, rank) + Sum.scratch(nw, rank)
    shape = lambda *dims: jax.ShapeDtypeStruct(dims, jnp.float32)
    return pl.pallas_call(
        functools.partial(fused, nz, nw, 3 * ITERS),
        out_shape=(shape(weeks, stores), shape(stores, rank), shape(weeks, rank)),
        in_specs=[pl.BlockSpec(memory_space=pltpu.VMEM)] * 5,
        out_specs=tuple([pl.BlockSpec(memory_space=pltpu.VMEM)] * 3),
        scratch_shapes=scratch,
        compiler_params=pltpu.CompilerParams(
            collective_id=0, has_side_effects=True, vmem_limit_bytes=48 * 1024 * 1024
        ),
    )(outcomes, observed_mask, store_region.reshape(1, stores), store_factor, week_factor)


def solution(mesh):
    placed = (
        P(("groups", "weeks"), "stores"),
        P(("groups", "weeks"), "stores"),
        P("stores"),
        P(("groups", "stores"), None),
        P(("groups", "weeks"), None),
    )
    return jax.shard_map(
        functools.partial(on_device, mesh.shape["stores"], mesh.shape["weeks"]),
        mesh=mesh,
        in_specs=placed,
        out_specs=(
            P(("groups", "weeks"), "stores"),
            P(("groups", "stores"), None),
            P(("groups", "weeks"), None),
        ),
        check_vma=False,
    )
```

time: 335 us -> 135 us (0.40); the launches traced: 329 us -> 135 us
  waiting for transfers between devices: 141 us -> 0 us
  Pallas kernels: 0 us -> 127 us
  other arithmetic: 95.4 us -> 0 us
  matrix products: 43.5 us -> 0 us
  blocking collectives: 33.2 us -> 0 us
  between operations: 14.7 us -> 0.65 us
  local copies, waits for them, and re-layouts: 0.65 us -> 7.77 us
    psum x4 -> x0, waiting for transfers between devices: 141 us -> none  [the longest x2 73.2 us: on_device(): lax.psum((local_product, jnp.dot(factor_week.T, factor_week, precision=PR...]
    pallas_call x0 -> x1, Pallas kernels: none -> 127 us  [on_device(): pl.pallas_call(functools.partial(fused, nz, nw, 3 * ITERS), out_shape=(sh...]
    another operation x20 -> x0, other arithmetic: 91.7 us -> none  [the longest x12 49.8 us: gram_inverse(): lower_factor = jnp.linalg.cholesky(gram + RIDGE_WEIGHT * identity)]
    dot_general x28 -> x0, matrix products: 42.3 us -> none  [the longest x4 6.26 us: masked_residual(): jnp.dot(factor_week, factor_store.T, precision=PRECISE)]
    psum x2 -> x0, blocking collectives: 33.2 us -> none  [the longest x1 23.1 us: on_device(): lax.psum((region_total, region_count), 'stores')]
    unnamed x30 -> x13, local copies, waits for them, and re-layouts: 0.29 us -> 7.77 us
    add x4 -> x0, other arithmetic: 3.69 us -> none  [gram_inverse(): lower_factor = jnp.linalg.cholesky(gram + RIDGE_WEIGHT * identity)]
  transfers between devices with their start and end apart: 4 -> 0, of which waited for: 4 -> 0; matrix products, arithmetic and copies ran while one was open for 0% -> 0% of each run, Pallas kernels for 0% -> 0%
where the time goes in v1:
time: 135 us
  Pallas kernels  127 us (94%)
  local copies, waits for them, and re-layouts  7.77 us (6%)
    pallas_call x1, Pallas kernels, on_device(): pl.pallas_call(functools.partial(fused, nz, nw, 3 * ITERS), out_shape=(sh...  127 us
    unnamed x13, local copies, waits for them, and re-layouts  7.77 us

profile of v1, /device:TPU:0, one launch (start us, length us, event | category | flops | bytes accessed | tf_op | source)
XLA Modules:
  0.0 135.2 jit_solution(18013582187296294459)
XLA Ops:
  0.6 0.0 copy-start
  0.6 1.2 copy-done
  1.9 0.0 copy-start.1
  1.9 1.2 copy-done.1
  3.1 0.0 copy-start.2
  3.1 1.2 copy-done.2
  4.3 0.0 copy-start.3
  4.3 0.8 copy-done.3
  5.1 0.0 copy-start.4
  5.2 0.7 copy-done.4
  5.8 126.7 %shard_map.76 = (f32[128,2048]{1,0:T(8,128)S(1)}, f32[2048,128]{1,0:T(8,128)S(1)}, f32[128,128]{1,0:T(8,128)S(1)}) custom-call(f32[128,2048]{1,0:T(8,128)S(1)} %copy-done, s32[128,2048]{1,0:T(8,128)S(1)} %copy-done.1, s32[1,2048]{1,0:T(1,128)S(1)} %bitcast.1, f32[2048,128]{1,0:T(8,128)S(1)} %copy-done.2, f32[128,128]{1,0:T(8,128)S(1)} %copy-done.3), custom_call_target="tpu_custom_call" | custom-call | tf_op jit(solution)/shard_map/pallas_call | solution.py:444
  132.6 1.0 copy.11
  133.6 1.0 copy.12
  134.5 0.6 copy.13
Async XLA Ops:
  0.6 1.2 copy-start
  1.9 1.2 copy-start.1
  3.1 1.2 copy-start.2
  4.3 0.8 copy-start.3
  5.1 0.7 copy-start.4

commit v2 on v1

--- a/solution.py
+++ b/solution.py
@@ -18,6 +18,23 @@
 def dot(a, b, ca=1, cb=0):
     return lax.dot_general(
         a, b, (((ca,), (cb,)), ((), ())), precision=PRECISE, preferred_element_type=jnp.float32
+    )
+
+
+def split(x):
+    high = x.astype(jnp.bfloat16)
+    return high, (x - high.astype(jnp.float32)).astype(jnp.bfloat16)
+
+
+def dot1(a, b, ca=1, cb=0):
+    return lax.dot_general(a, b, (((ca,), (cb,)), ((), ())), preferred_element_type=jnp.float32)
+
+
+def dot3(a, b, ca=1, cb=0):
+    a_high, a_low = split(a)
+    b_high, b_low = split(b)
+    return (
+        dot1(a_high, b_high, ca, cb) + dot1(a_high, b_low, ca, cb) + dot1(a_low, b_high, ca, cb)
     )
 
 
@@ -32,12 +49,16 @@
     def step(_, carry):
         matrix = work[...]
         panel = matrix[:PANEL, :]
-        for j in range(PANEL):
-            pivot = 1.0 / panel[j : j + 1, j : j + 1]
-            row = jnp.where(panel_lane[:1] == j, pivot, panel[j : j + 1, :] * pivot)
-            column = panel[:, j : j + 1]
-            cleared = jnp.where(panel_lane == j, 0.0, panel)
-            panel = jnp.where(panel_row == j, row, cleared - column * row)
+        columns = [jnp.broadcast_to(panel[:, j : j + 1], panel.shape) for j in range(PANEL)]
+        for k in range(PANEL):
+            pivot = 1.0 / columns[k][k : k + 1, :]
+            column = columns[k]
+            row = jnp.where(panel_lane[:1] == k, pivot, panel[k : k + 1, :] * pivot)
+            cleared = jnp.where(panel_lane == k, 0.0, panel)
+            panel = jnp.where(panel_row == k, row, cleared - column * row)
+            for j in range(k + 1, PANEL):
+                scaled = columns[j][k : k + 1, :] * pivot
+                columns[j] = jnp.where(panel_row == k, scaled, columns[j] - column * scaled)
         rest = matrix[PANEL:, :]
         kept = jnp.where(lane_at[PANEL:] < PANEL, 0.0, rest)
         rest = kept - dot(rest[:, :PANEL], panel)
@@ -124,8 +145,17 @@
 
 
 def fused(nz, nw, n_sum, *refs):
-    (outcomes, mask, region, a_first, b_first, imputed, a_out, b_out) = refs[:8]
-    refs = refs[8:]
+    hbm_in, hbm_out = refs[:5], refs[5:8]
+    (outcomes, mask, region, a_first, b_first, imputed, b_last, in_sems, out_sems) = refs[8:17]
+    refs = refs[17:]
+    loads = [
+        pltpu.make_async_copy(source, target, in_sems.at[k])
+        for k, (source, target) in enumerate(
+            zip(hbm_in, (outcomes, mask, region, a_first, b_first))
+        )
+    ]
+    for k in (2, 1, 0, 3, 4):
+        loads[k].start()
     (onehot, obs, cent, base, pred, obs_t, cent_t, work, region_buf, store_buf, effect_row,
      region_sems, store_sems) = refs[:13]
     refs = refs[13:]
@@ -143,24 +173,30 @@
     core, chip, chips = lax.rem(w, 2), w // 2, nw // 2
     half = stores // 2
     sub = half // chips
-    tile = 128
+    tile = min(256, sub)
     per_sub = sub // tile
     n_tiles = half // tile
     n_away = n_tiles - per_sub
     wide = stores // 4
-
+    big = stores // 2
+    step = stores // 4
+
+    b_store = pltpu.make_async_copy(b_last, hbm_out[2], out_sems.at[0])
     barrier = pltpu.get_barrier_semaphore()
     for j in range(1, nz):
         pl.semaphore_signal(barrier, device_id={"stores": lax.rem(z + j, nz)}, device_id_type=MESH)
     for j in range(1, nw):
         pl.semaphore_signal(barrier, device_id={"weeks": lax.rem(w + j, nw)}, device_id_type=MESH)
 
+    for k in (2, 1, 0):
+        loads[k].wait()
     onehot[...] = (
         lax.broadcasted_iota(jnp.int32, (REGIONS, stores), 0) == region[...]
-    ).astype(jnp.float32)
+    ).astype(jnp.bfloat16)
     obs[...] = mask[...].astype(jnp.float32)
-    total = dot(onehot[...], obs[...] * outcomes[...], 1, 1)
-    count = dot(onehot[...], obs[...], 1, 1)
+    high, low = split(obs[...] * outcomes[...])
+    total = dot1(onehot[...], high, 1, 1) + dot1(onehot[...], low, 1, 1)
+    count = dot1(onehot[...], obs[...].astype(jnp.bfloat16), 1, 1)
     region_buf[0] = jnp.concatenate([total, count], axis=0)
     pl.semaphore_wait(barrier, nz + nw - 2)
 
@@ -173,14 +209,14 @@
     for j in range(1, nz):
         region_copy(j).start()
 
-    def gram_of(ref):
-        def body(t, total):
-            block = ref[pl.ds(pl.multiple_of(t * 256, 256), 256), :]
-            return total + dot(block.T, block)
-
-        return lax.fori_loop(0, stores // 256, body, jnp.zeros((rank, rank), jnp.float32))
-
-    sums[0].start(gram_of(a_first))
+    def gram_step(t, total):
+        block = a_first[pl.ds(pl.multiple_of(t * big, big), big), :]
+        return total + dot3(block, block, 0, 0)
+
+    loads[3].wait()
+    loads[4].wait()
+    zero = jnp.zeros((rank, rank), jnp.float32)
+    sums[0].start(lax.fori_loop(0, stores // big, gram_step, zero))
 
     for j in range(1, nz):
         region_copy(j).wait_recv()
@@ -192,7 +228,8 @@
         0, nz, add_region, jnp.zeros(region_buf.shape[1:], jnp.float32)
     )
     effect = (sums_region[:REGIONS] / (sums_region[REGIONS:] + 1.0)).T
-    base[...] = dot(effect, onehot[...])
+    high, low = split(effect)
+    base[...] = dot1(high, onehot[...]) + dot1(low, onehot[...])
     store_total = jnp.sum(obs[...] * (outcomes[...] - base[...]), axis=0, keepdims=True)
     store_count = jnp.sum(obs[...], axis=0, keepdims=True)
     for q in range(4):
@@ -209,23 +246,22 @@
         store_copy(j).start()
     sums[0].spread()
 
-    def predict(b_value, ref):
-        def body(t, carry):
-            at = pl.ds(pl.multiple_of(t * 256, 256), 256)
-            pred[:, at] = dot(b_value, ref[at, :], 1, 1)
-            return carry
-
-        lax.fori_loop(0, stores // 256, body, 0)
-
-    predict(b_first[...], a_first)
+    b_value = b_first[...]
+
+    def predict_step(t, carry):
+        at = pl.ds(pl.multiple_of(t * step, step), step)
+        pred[:, at] = dot3(b_value, a_first[at, :], 1, 1)
+        return carry
+
+    lax.fori_loop(0, stores // step, predict_step, 0)
 
     def turn(source, target):
         def body(t, carry):
-            at = pl.ds(pl.multiple_of(t * 128, 128), 128)
+            at = pl.ds(pl.multiple_of(t * step, step), step)
             target[at, :] = source[:, at].T
             return carry
 
-        lax.fori_loop(0, stores // 128, body, 0)
+        lax.fori_loop(0, stores // step, body, 0)
 
     turn(obs, obs_t)
     for j in range(1, nw):
@@ -241,22 +277,20 @@
     base[...] = base[...] + effect_row[...]
     cent[...] = obs[...] * (outcomes[...] - base[...])
 
-    b_value = b_first[...]
+    def product_step(t, total):
+        at = pl.ds(pl.multiple_of(t * big, big), big)
+        residual = cent[:, at] - obs[:, at] * pred[:, at]
+        return total + dot3(residual, a_first[at, :])
+
+    product = lax.fori_loop(
+        0, stores // big, product_step, jnp.zeros((weeks, rank), jnp.float32)
+    )
+    gram = None
     a_ref = a_first
     for it in range(ITERS):
         sum_gram, sum_product, sum_week = sums[3 * it : 3 * it + 3]
         if it > 0:
-            sum_gram.start(gram_of(a_ref))
-            predict(b_value, a_ref)
-
-        def product_step(t, total):
-            at = pl.ds(pl.multiple_of(t * 256, 256), 256)
-            residual = cent[:, at] - obs[:, at] * pred[:, at]
-            return total + dot(residual, a_ref[at, :])
-
-        product = lax.fori_loop(
-            0, stores // 256, product_step, jnp.zeros((weeks, rank), jnp.float32)
-        )
+            sum_gram.start(gram)
         if weeks < rank:
             product = jnp.concatenate(
                 [product, jnp.zeros((rank - weeks, rank), jnp.float32)], axis=0
@@ -280,8 +314,8 @@
 
         def local_product(row):
             at = pl.ds(pl.multiple_of(row, tile), tile)
-            predicted = dot(a_ref[at, :], b_value, 1, 1)
-            return dot(cent_t[at, :] - obs_t[at, :] * predicted, b_value)
+            predicted = dot3(a_ref[at, :], b_value, 1, 1)
+            return dot3(cent_t[at, :] - obs_t[at, :] * predicted, b_value)
 
         def sib_copy(i):
             at = pl.ds(rows_of(i), tile)
@@ -355,26 +389,49 @@
                 x_copy(i).wait_recv()
                 total = total + x_recv[it, pl.ds(pl.multiple_of(i * tile, tile), tile)]
             rows = pl.ds(pl.multiple_of(core * half + chip * sub + q * tile, tile), tile)
-            a_all[it, rows] = dot(total + dot(a_ref[rows, :], week_gram), inv)
+            a_all[it, rows] = dot3(total + dot3(a_ref[rows, :], week_gram), inv)
             for d in range(1, chips):
                 a_copy_x(d, q, False).start()
             a_copy_sib(0, q, False).start()
             return carry
 
-        def forward(q, carry):
-            for d in range(1, chips):
-                a_copy_x(d, q, True).wait_recv()
-                a_copy_sib(d, q, False).start()
-            return carry
-
-        def arrive(q, carry):
-            for d in range(chips):
-                a_copy_sib(d, q, True).wait_recv()
-            return carry
-
         lax.fori_loop(0, per_sub, update, 0)
-        lax.fori_loop(0, per_sub, forward, 0)
-        lax.fori_loop(0, per_sub, arrive, 0)
+        last = it == ITERS - 1
+        if last:
+            b_last[...] = b_value
+            b_store.start()
+        product = jnp.zeros((weeks, rank), jnp.float32)
+        gram = jnp.zeros((rank, rank), jnp.float32)
+        stored = []
+        for d in range(chips):
+            owner = lax.rem(chip + chips - d, chips)
+            for own_part in (True, False):
+                for q in range(per_sub):
+                    if not own_part:
+                        a_copy_sib(d, q, True).wait_recv()
+                    elif d > 0:
+                        a_copy_x(d, q, True).wait_recv()
+                        a_copy_sib(d, q, False).start()
+                part = core if own_part else 1 - core
+                at = pl.ds(pl.multiple_of(part * half + owner * sub, sub), sub)
+                block = a_all[it, at]
+                predicted = dot3(b_value, block, 1, 1)
+                if last:
+                    k = 2 * d + 1 - int(own_part)
+                    imputed[:, at] = base[:, at] + predicted
+                    stored += [
+                        pltpu.make_async_copy(
+                            imputed.at[:, at], hbm_out[0].at[:, at], out_sems.at[2 * k + 1]
+                        ),
+                        pltpu.make_async_copy(
+                            a_all.at[it, at], hbm_out[1].at[at], out_sems.at[2 * k + 2]
+                        ),
+                    ]
+                    stored[-2].start()
+                    stored[-1].start()
+                else:
+                    gram = gram + dot3(block, block, 0, 0)
+                    product = product + dot3(cent[:, at] - obs[:, at] * predicted, block)
 
         def drain_tiles(i, carry):
             sib_copy(i).wait_send()
@@ -396,22 +453,15 @@
         lax.fori_loop(0, per_sub, drain_rows, 0)
         a_ref = a_all.at[it]
 
-    b_out[...] = b_value
-
-    def finish(t, carry):
-        at = pl.ds(pl.multiple_of(t * 256, 256), 256)
-        block = a_ref[at, :]
-        a_out[at, :] = block
-        imputed[:, at] = base[:, at] + dot(b_value, block, 1, 1)
-        return carry
-
-    lax.fori_loop(0, stores // 256, finish, 0)
     for j in range(1, nz):
         region_copy(j).wait_send()
     for j in range(1, nw):
         store_copy(j).wait_send()
     for item in sums:
         item.drain()
+    for copy in stored:
+        copy.wait()
+    b_store.wait()
 
 
 def on_device(nz, nw, outcomes, observed_mask, store_region, store_factor, week_factor):
@@ -419,13 +469,18 @@
     rank = week_factor.shape[1]
     chips = nw // 2
     half = stores // 2
-    n_tiles = half // 128
+    away = max(half - half // chips, 128)
+    tile = min(256, half // chips)
+    n_tiles = half // tile
     per_sub = n_tiles // chips
-    away = max(half - half // chips, 128)
     vmem = lambda *shape: pltpu.VMEM(shape, jnp.float32)
     sems = lambda *shape: pltpu.SemaphoreType.DMA(shape)
     scratch = [
-        vmem(REGIONS, stores),
+        vmem(weeks, stores), pltpu.VMEM((weeks, stores), jnp.int32),
+        pltpu.VMEM((1, stores), jnp.int32),
+        vmem(stores, rank), vmem(weeks, rank), vmem(weeks, stores), vmem(weeks, rank),
+        sems(5), sems(4 * chips + 1),
+        pltpu.VMEM((REGIONS, stores), jnp.bfloat16),
         vmem(weeks, stores), vmem(weeks, stores), vmem(weeks, stores), vmem(weeks, stores),
         vmem(stores, weeks), vmem(stores, weeks),
         vmem(rank, rank),
@@ -444,11 +499,11 @@
     return pl.pallas_call(
         functools.partial(fused, nz, nw, 3 * ITERS),
         out_shape=(shape(weeks, stores), shape(stores, rank), shape(weeks, rank)),
-        in_specs=[pl.BlockSpec(memory_space=pltpu.VMEM)] * 5,
-        out_specs=tuple([pl.BlockSpec(memory_space=pltpu.VMEM)] * 3),
+        in_specs=[pl.BlockSpec(memory_space=pltpu.HBM)] * 5,
+        out_specs=tuple([pl.BlockSpec(memory_space=pltpu.HBM)] * 3),
         scratch_shapes=scratch,
         compiler_params=pltpu.CompilerParams(
-            collective_id=0, has_side_effects=True, vmem_limit_bytes=48 * 1024 * 1024
+            collective_id=0, has_side_effects=True, vmem_limit_bytes=56 * 1024 * 1024
         ),
     )(outcomes, observed_mask, store_region.reshape(1, stores), store_factor, week_factor)
 

time: 135 us -> 88.5 us (0.66)
  Pallas kernels: 127 us -> 83.2 us
  local copies, waits for them, and re-layouts: 7.77 us -> 3.99 us
    pallas_call x1, Pallas kernels: 127 us -> 83.2 us  [on_device(): pl.pallas_call(functools.partial(fused, nz, nw, 3 * ITERS), out_shape=(sh...]
    unnamed x13 -> x7, local copies, waits for them, and re-layouts: 7.77 us -> 3.99 us
where the time goes in v2:
time: 88.5 us; the launch traced here: 87.8 us
  Pallas kernels  83.2 us (94%)
  local copies, waits for them, and re-layouts  3.99 us (5%)
    pallas_call x1, Pallas kernels, on_device(): pl.pallas_call(functools.partial(fused, nz, nw, 3 * ITERS), out_shape=(sh...  83.2 us
    unnamed x7, local copies, waits for them, and re-layouts  3.99 us

profile of v2, /device:TPU:0, one launch (start us, length us, event | category | flops | bytes accessed | tf_op | source)
XLA Modules:
  0.0 87.8 jit_solution(517209772676736315)
XLA Ops:
  0.6 83.2 %shard_map.76 = (f32[128,2048]{1,0:T(8,128)}, f32[2048,128]{1,0:T(8,128)}, f32[128,128]{1,0:T(8,128)}) custom-call(f32[128,2048]{1,0:T(8,128)} %refs_0_.1, s32[128,2048]{1,0:T(8,128)} %refs_1_.1, s32[1,2048]{1,0:T(1,128)} %bitcast.1, f32[2048,128]{1,0:T(8,128)} %refs_3_.1, f32[128,128]{1,0:T(8,128)} %refs_4_.1), custom_call_target="tpu_custom_call" | custom-call | tf_op jit(solution)/shard_map/pallas_call | solution.py:499
  83.8 0.0 copy-start
  83.8 2.4 %copy.11 = f32[128,2048]{1,0:T(8,128)} copy(f32[128,2048]{1,0:T(8,128)} %get-tuple-element.6) | data formatting | bytes 2097152
  86.2 0.0 copy-done
  86.2 0.0 copy-start.1
  86.2 1.0 %copy.12 = f32[2048,128]{1,0:T(8,128)} copy(f32[2048,128]{1,0:T(8,128)S(1)} %copy-done) | data formatting | bytes 2097152
  87.2 0.0 copy-done.1
  87.2 0.6 copy.13
Async XLA Ops:
  83.8 2.4 %copy-start = (f32[2048,128]{1,0:T(8,128)S(1)}, f32[2048,128]{1,0:T(8,128)}, u32[]{:S(2)}) copy-start(f32[2048,128]{1,0:T(8,128)} %get-tuple-element.7) | copy-start | bytes 3145732
  86.2 1.0 %copy-start.1 = (f32[128,128]{1,0:T(8,128)S(1)}, f32[128,128]{1,0:T(8,128)}, u32[]{:S(2)}) copy-start(f32[128,128]{1,0:T(8,128)} %get-tuple-element.8) | copy-start | bytes 196612

commit v3 on v2

--- a/solution.py
+++ b/solution.py
@@ -145,9 +145,9 @@
 
 
 def fused(nz, nw, n_sum, *refs):
-    hbm_in, hbm_out = refs[:5], refs[5:8]
-    (outcomes, mask, region, a_first, b_first, imputed, b_last, in_sems, out_sems) = refs[8:17]
-    refs = refs[17:]
+    hbm_in, (imputed, a_out, b_out) = refs[:5], refs[5:8]
+    (outcomes, mask, region, a_first, b_first, in_sems) = refs[8:14]
+    refs = refs[14:]
     loads = [
         pltpu.make_async_copy(source, target, in_sems.at[k])
         for k, (source, target) in enumerate(
@@ -181,7 +181,6 @@
     big = stores // 2
     step = stores // 4
 
-    b_store = pltpu.make_async_copy(b_last, hbm_out[2], out_sems.at[0])
     barrier = pltpu.get_barrier_semaphore()
     for j in range(1, nz):
         pl.semaphore_signal(barrier, device_id={"stores": lax.rem(z + j, nz)}, device_id_type=MESH)
@@ -356,8 +355,8 @@
 
         lax.fori_loop(0, n_away, to_sibling, 0)
         lax.fori_loop(0, n_away, to_chips, 0)
+        lax.fori_loop(n_away, n_tiles, to_sibling, 0)
         sum_week.spread()
-        lax.fori_loop(n_away, n_tiles, to_sibling, 0)
         lax.fori_loop(n_away, n_tiles, keep, 0)
         week_gram = sum_week.result()
         inv = inverse(week_gram, work)
@@ -398,11 +397,9 @@
         lax.fori_loop(0, per_sub, update, 0)
         last = it == ITERS - 1
         if last:
-            b_last[...] = b_value
-            b_store.start()
+            b_out[...] = b_value
         product = jnp.zeros((weeks, rank), jnp.float32)
         gram = jnp.zeros((rank, rank), jnp.float32)
-        stored = []
         for d in range(chips):
             owner = lax.rem(chip + chips - d, chips)
             for own_part in (True, False):
@@ -417,18 +414,8 @@
                 block = a_all[it, at]
                 predicted = dot3(b_value, block, 1, 1)
                 if last:
-                    k = 2 * d + 1 - int(own_part)
                     imputed[:, at] = base[:, at] + predicted
-                    stored += [
-                        pltpu.make_async_copy(
-                            imputed.at[:, at], hbm_out[0].at[:, at], out_sems.at[2 * k + 1]
-                        ),
-                        pltpu.make_async_copy(
-                            a_all.at[it, at], hbm_out[1].at[at], out_sems.at[2 * k + 2]
-                        ),
-                    ]
-                    stored[-2].start()
-                    stored[-1].start()
+                    a_out[at, :] = block
                 else:
                     gram = gram + dot3(block, block, 0, 0)
                     product = product + dot3(cent[:, at] - obs[:, at] * predicted, block)
@@ -459,9 +446,6 @@
         store_copy(j).wait_send()
     for item in sums:
         item.drain()
-    for copy in stored:
-        copy.wait()
-    b_store.wait()
 
 
 def on_device(nz, nw, outcomes, observed_mask, store_region, store_factor, week_factor):
@@ -478,8 +462,8 @@
     scratch = [
         vmem(weeks, stores), pltpu.VMEM((weeks, stores), jnp.int32),
         pltpu.VMEM((1, stores), jnp.int32),
-        vmem(stores, rank), vmem(weeks, rank), vmem(weeks, stores), vmem(weeks, rank),
-        sems(5), sems(4 * chips + 1),
+        vmem(stores, rank), vmem(weeks, rank),
+        sems(5),
         pltpu.VMEM((REGIONS, stores), jnp.bfloat16),
         vmem(weeks, stores), vmem(weeks, stores), vmem(weeks, stores), vmem(weeks, stores),
         vmem(stores, weeks), vmem(stores, weeks),
@@ -500,10 +484,10 @@
         functools.partial(fused, nz, nw, 3 * ITERS),
         out_shape=(shape(weeks, stores), shape(stores, rank), shape(weeks, rank)),
         in_specs=[pl.BlockSpec(memory_space=pltpu.HBM)] * 5,
-        out_specs=tuple([pl.BlockSpec(memory_space=pltpu.HBM)] * 3),
+        out_specs=tuple([pl.BlockSpec(memory_space=pltpu.VMEM)] * 3),
         scratch_shapes=scratch,
         compiler_params=pltpu.CompilerParams(
-            collective_id=0, has_side_effects=True, vmem_limit_bytes=56 * 1024 * 1024
+            collective_id=0, has_side_effects=True, vmem_limit_bytes=48 * 1024 * 1024
         ),
     )(outcomes, observed_mask, store_region.reshape(1, stores), store_factor, week_factor)
 

time: 88.5 us -> 91.8 us (1.037)
  local copies, waits for them, and re-layouts: 3.99 us -> 7.77 us
    unnamed x7 -> x13, local copies, waits for them, and re-layouts: 3.99 us -> 7.77 us
where the time goes in v3:
time: 91.8 us; the launch traced here: 91.3 us
  Pallas kernels  82.9 us (90%)
  local copies, waits for them, and re-layouts  7.77 us (8%)
    pallas_call x1, Pallas kernels, on_device(): pl.pallas_call(functools.partial(fused, nz, nw, 3 * ITERS), out_shape=(sh...  82.9 us
    unnamed x13, local copies, waits for them, and re-layouts  7.77 us

profile of v3, /device:TPU:0, one launch (start us, length us, event | category | flops | bytes accessed | tf_op | source)
XLA Modules:
  0.0 91.3 jit_solution(6929577348163420578)
XLA Ops:
  0.6 0.0 copy-start
  0.6 1.2 %copy-done = f32[128,2048]{1,0:T(8,128)S(1)} copy-done((f32[128,2048]{1,0:T(8,128)S(1)}, f32[128,2048]{1,0:T(8,128)}, u32[]{:S(2)}) %copy-start) | copy-done | bytes 1048600
  1.9 0.0 copy-start.1
  1.9 1.2 %copy-done.1 = s32[128,2048]{1,0:T(8,128)S(1)} copy-done((s32[128,2048]{1,0:T(8,128)S(1)}, s32[128,2048]{1,0:T(8,128)}, u32[]{:S(2)}) %copy-start.1) | copy-done | bytes 1048600
  3.1 0.0 copy-start.2
  3.1 1.2 %copy-done.2 = f32[2048,128]{1,0:T(8,128)S(1)} copy-done((f32[2048,128]{1,0:T(8,128)S(1)}, f32[2048,128]{1,0:T(8,128)}, u32[]{:S(2)}) %copy-start.2) | copy-done | bytes 1048600
  4.3 0.0 copy-start.3
  4.3 0.8 copy-done.3
  5.1 0.0 copy-start.4
  5.2 0.7 copy-done.4
  5.8 82.9 %shard_map.76 = (f32[128,2048]{1,0:T(8,128)S(1)}, f32[2048,128]{1,0:T(8,128)S(1)}, f32[128,128]{1,0:T(8,128)S(1)}) custom-call(f32[128,2048]{1,0:T(8,128)S(1)} %copy-done, s32[128,2048]{1,0:T(8,128)S(1)} %copy-done.1, s32[1,2048]{1,0:T(1,128)S(1)} %bitcast.1, f32[2048,128]{1,0:T(8,128)S(1)} %copy-done.2, f32[128,128]{1,0:T(8,128)S(1)} %copy-done.3), custom_call_target="tpu_custom_call" | custom-call | tf_op jit(solution)/shard_map/pallas_call | solution.py:483
  88.7 1.0 %copy.11 = f32[128,2048]{1,0:T(8,128)} copy(f32[128,2048]{1,0:T(8,128)S(1)} %get-tuple-element.6) | data formatting | bytes 2097152
  89.7 1.0 %copy.12 = f32[2048,128]{1,0:T(8,128)} copy(f32[2048,128]{1,0:T(8,128)S(1)} %get-tuple-element.7) | data formatting | bytes 2097152
  90.7 0.6 copy.13
Async XLA Ops:
  0.6 1.2 %copy-start = (f32[128,2048]{1,0:T(8,128)S(1)}, f32[128,2048]{1,0:T(8,128)}, u32[]{:S(2)}) copy-start(f32[128,2048]{1,0:T(8,128)} %refs_0_.1) | copy-start | bytes 3145732
  1.9 1.2 %copy-start.1 = (s32[128,2048]{1,0:T(8,128)S(1)}, s32[128,2048]{1,0:T(8,128)}, u32[]{:S(2)}) copy-start(s32[128,2048]{1,0:T(8,128)} %refs_1_.1) | copy-start | bytes 3145732
  3.1 1.2 %copy-start.2 = (f32[2048,128]{1,0:T(8,128)S(1)}, f32[2048,128]{1,0:T(8,128)}, u32[]{:S(2)}) copy-start(f32[2048,128]{1,0:T(8,128)} %refs_3_.1) | copy-start | bytes 3145732
  4.3 0.8 copy-start.3
  5.1 0.7 copy-start.4
